TPU v7x, 128 devices: a whole 4x4x4 slice. The times are simulated.
128 devices in a mesh: grp: 8 (over x, core), tile: 16 (over y, z).
Axes of the slice: x: 4, y: 4, z: 4, core: 2. Of those that a mesh axis runs over, the one named last changes fastest.
Arguments:
- molecule_coords: float32 [3, 2097152], P(None, ('grp', 'tile')), may hold values from 0 to 1.6
- molecule_speeds: float32 [3, 2097152], P(None, ('grp', 'tile')), may hold values from -6 to 6
- molecule_thermal_state: float32 [2097152], P(('grp', 'tile')), may hold values from 0.5 to 2
- conservative_strength: float32 [2097152], P(('grp', 'tile')), may hold values from 0.05 to 0.5
- noise_keys: int32 [2097152], P(('grp', 'tile')), may hold values from 0 to 32767
- exported_tile_places: int32 [128, 16, 12], P(('grp', 'tile')), may hold values from 0 to 127
- tile_couplings: int32 [128, 1024, 2], P(('grp', 'tile')), may hold values from 0 to 383, as said below
- processor_coupling_tally: int32 [128], P(('grp', 'tile')), may hold values from 512 to 1024
Outputs:
- force_heat: float32 [4, 2097152], P(None, ('grp', 'tile'))
Inputs may be any that keep to these rules, and one draw needn't show every extreme that they name: `tile_couplings`: second slots of workers in the lowest slab are below 192; first slots are below 192.
All inputs are finite; a program needn't handle non-finite values.
Results may differ from a plain program's by a relative error of at most 0.0003.
Values sent between devices are 32-bit elements; how exact they have to be, the bound alone decides.
A program may use at most 128 MiB of HBM per device.

v0:
```python
import math
import jax
import jax.numpy as jnp
from jax import lax
from jax.sharding import PartitionSpec as P

friction = 0.45
noise_amp = 0.3
conductivity = 0.1


def passed_along(value, axis, steps):
    count = lax.axis_size(axis)
    leading, last = (max(0, -steps), min(count, count - steps))
    return lax.ppermute(value, axis, [(source, source + steps) for source in range(leading, last)])


def tile_pair(first, second):
    offset = first[0:3, :, None] - second[0:3, None, :]
    radius = jnp.sqrt(jnp.sum(offset * offset, 0) + 0.01)
    unit = offset / radius
    weight = jnp.maximum(1.0 - radius, 0.0)
    relative = first[3:6, :, None] - second[3:6, None, :]
    along = jnp.sum(unit * relative, 0)
    repulse = 0.5 * (first[7][:, None] + second[7][None, :])
    seed_first = first[8].astype(jnp.int32)
    seed_second = second[8].astype(jnp.int32)
    hashed = (
        seed_first[:, None] * seed_second[None, :] + seed_first[:, None] + seed_second[None, :]
    ) % 65521
    noise = hashed.astype(jnp.float32) * (2.0 / 65521.0) - 1.0
    magnitude = repulse * weight - friction * weight * weight * along + noise_amp * weight * noise
    force = magnitude[None] * unit
    conduct = conductivity * weight * weight * (second[6][None, :] - first[6][:, None])
    viscous = 0.5 * friction * weight * weight * along * along
    on_first = jnp.concatenate([jnp.sum(force, 2), jnp.sum(conduct + viscous, 1)[None]], 0)
    on_second = jnp.concatenate([-jnp.sum(force, 1), jnp.sum(viscous - conduct, 0)[None]], 0)
    return (on_first, on_second)


def tile_self(block_data):
    offset = block_data[0:3, :, None] - block_data[0:3, None, :]
    radius = jnp.sqrt(jnp.sum(offset * offset, 0) + 0.01)
    unit = offset / radius
    weight = jnp.maximum(1.0 - radius, 0.0)
    relative = block_data[3:6, :, None] - block_data[3:6, None, :]
    along = jnp.sum(unit * relative, 0)
    repulse = 0.5 * (block_data[7][:, None] + block_data[7][None, :])
    seed_first = block_data[8].astype(jnp.int32)
    hashed = (
        seed_first[:, None] * seed_first[None, :] + seed_first[:, None] + seed_first[None, :]
    ) % 65521
    noise = hashed.astype(jnp.float32) * (2.0 / 65521.0) - 1.0
    others = 1.0 - jnp.eye(block_data.shape[1], dtype=jnp.float32)
    magnitude = (
        repulse * weight - friction * weight * weight * along + noise_amp * weight * noise
    ) * others
    force = magnitude[None] * unit
    conduct = conductivity * weight * weight * (block_data[6][None, :] - block_data[6][:, None])
    viscous = 0.5 * friction * weight * weight * along * along
    heating = jnp.sum((conduct + viscous) * others, 1)
    return jnp.concatenate([jnp.sum(force, 2), heating[None]], 0)


def one_hot(indices, count):
    return (indices[:, None] == jnp.arange(count, dtype=jnp.int32)[None, :]).astype(jnp.float32)


def per_device(
    molecule_coords,
    molecule_speeds,
    molecule_thermal_state,
    conservative_strength,
    noise_keys,
    exported_tile_places,
    tile_couplings,
    processor_coupling_tally,
):
    n_tile = lax.axis_size("tile")
    blocks = molecule_coords.shape[1] // 128
    slot_table = exported_tile_places[0]
    cap = slot_table.shape[1]
    buffer_len = n_tile * cap
    owned = jnp.concatenate(
        [
            molecule_coords,
            molecule_speeds,
            molecule_thermal_state[None],
            conservative_strength[None],
            noise_keys[None].astype(jnp.float32),
        ],
        0,
    )
    owned = owned.reshape(9, blocks, 128).transpose(1, 0, 2)
    group_data = lax.all_gather(owned, "tile", axis=0, tiled=True)
    tables = lax.all_gather(exported_tile_places, "tile", axis=0, tiled=True)
    my_index = lax.axis_index("tile")
    my_slots = lax.dynamic_index_in_dim(tables, my_index, 1, keepdims=False)
    group_ids = (jnp.arange(n_tile, dtype=jnp.int32)[:, None] * blocks + my_slots).reshape(-1)
    held_blocks = group_data[group_ids]
    neighbour = passed_along(held_blocks, "grp", 1)
    reachable = jnp.concatenate([held_blocks, neighbour], 0)
    total_pair_count = tile_couplings.shape[1]
    batch = math.gcd(total_pair_count, 64)
    first_slots = tile_couplings[0, :, 0].reshape(-1, batch)
    second_slots = tile_couplings[0, :, 1].reshape(-1, batch)
    live_rows = (
        (jnp.arange(total_pair_count, dtype=jnp.int32) < processor_coupling_tally[0])
        .astype(jnp.float32)
        .reshape(-1, batch)
    )

    def consume(carry, items):
        near_acc, far_acc = carry
        first_idx, second_index, live = items
        on_first, on_second = jax.vmap(tile_pair)(held_blocks[first_idx], reachable[second_index])
        on_first = (on_first * live[:, None, None]).reshape(batch, 512)
        on_second = (on_second * live[:, None, None]).reshape(batch, 512)
        near_acc = near_acc + jnp.dot(
            one_hot(first_idx, buffer_len).T, on_first, precision=lax.Precision.HIGHEST
        )
        far_acc = far_acc + jnp.dot(
            one_hot(second_index, 2 * buffer_len).T, on_second, precision=lax.Precision.HIGHEST
        )
        return ((near_acc, far_acc), None)

    start_carry = (
        jnp.zeros((buffer_len, 512), jnp.float32),
        jnp.zeros((2 * buffer_len, 512), jnp.float32),
    )
    (near_acc, far_acc), _ = lax.scan(consume, start_carry, (first_slots, second_slots, live_rows))
    lower_terms = passed_along(far_acc[buffer_len:], "grp", -1)
    own_total = near_acc + far_acc[:buffer_len] + lower_terms
    selector = one_hot(group_ids, n_tile * blocks)
    summed = lax.psum_scatter(
        jnp.dot(selector.T, own_total, precision=lax.Precision.HIGHEST),
        "tile",
        scatter_dimension=0,
        tiled=True,
    )
    self_batch = math.gcd(blocks, 16)

    def self_step(carry, group_data):
        return (carry, jax.vmap(tile_self)(group_data))

    _, selfs = lax.scan(
        self_step, jnp.zeros((), jnp.float32), owned.reshape(-1, self_batch, 9, 128)
    )
    result = summed.reshape(blocks, 4, 128) + selfs.reshape(blocks, 4, 128)
    return result.transpose(1, 0, 2).reshape(4, blocks * 128)


def solution(mesh):
    in_specs = (
        P(None, ("grp", "tile")),
        P(None, ("grp", "tile")),
        P(("grp", "tile")),
        P(("grp", "tile")),
        P(("grp", "tile")),
        P(("grp", "tile"), None, None),
        P(("grp", "tile"), None, None),
        P(("grp", "tile")),
    )
    out_specs = P(None, ("grp", "tile"))
    return jax.shard_map(
        per_device, mesh=mesh, in_specs=in_specs, out_specs=out_specs, check_vma=False
    )
```

profile of v0, /device:TPU:0, one launch (start us, length us, event | category | flops | bytes accessed | tf_op | source)
XLA Modules:
  0.0 833.5 jit_solution(1761941762387604038)
XLA Ops:
  12.7 25.4 %all_gather.6 = s32[16,16,12]{2,1,0:T(8,128)S(1)} all-gather(s32[1,16,12]{2,1,0:T(8,128)S(1)} %copy.32), channel_id=1, replica_groups=mesh['grp'=8,'tile'=16] {'tile'}, dimensions={0}, use_global_device_ids=true | all-gather | bytes 13056 | tf_op jit(solution)/shard_map/all_gather | solution.py:96
  40.1 50.3 %all-gather.2.cloned.1.call-done = f32[2048,9,128]{2,0,1:T(8,128)} async-done(((f32[128,9,128]{2,0,1:T(8,128)}), f32[2048,9,128]{2,0,1:T(8,128)}) %all-gather.2.cloned.1.call-update) | async-done | bytes 9437200 | tf_op jit(solution)/shard_map/all_gather | solution.py:95
  90.5 12.8 %copy.33 = f32[2048,9,128]{2,1,0:T(8,128)} copy(f32[2048,9,128]{2,0,1:T(8,128)} %all-gather.2.cloned.1.call-done) | data formatting | bytes 18874368 | tf_op jit(solution)/shard_map/all_gather | solution.py:95
  117.3 606.1 %while.28 = (s32[]{:T(128)}, f32[192,512]{1,0:T(8,128)}, f32[384,512]{1,0:T(8,128)S(1)}, s32[16,64]{1,0:T(8,128)S(1)}, f32[192,9,128]{2,1,0:T(8,128)S(1)}, /*ind...) while((s32[]{:T(128)}, f32[192,512]{1,0:T(8,128)}, ...), condition=%wide.region_7.8_spmd.clone, body=%wide.region_0.7_spmd.clone.sunk | while | flops 305871232 | bytes 52507452 | solution.py:131
  126.5 8.0 multiply_reduce_fusion.11
  134.7 9.2 %subtract_reduce_fusion.2 = (f32[64,128]{1,0:T(8,128)S(1)}, f32[64,128]{1,0:T(8,128)S(1)}, f32[64,128,128]{2,1,0:T(8,128)S(1)}) fusion(f32[64,128,128]{2,1,0:T(8,128)S(1)} %multiply_reduce_fusion.11, f32[64,128]{1,0:T(8,128)S(1)} %bitcast.118, f32[64,128]{1,0:T(8,128)S(1)} %bitcast.115, f32[64,128,128]{2,1,0:T(8,128)S(1)} %fusion.72, ...), kind=kLoop, calls=%fused_computation.59.clone.1 | loop fusion | flops 38780928 | bytes 12845056 | tf_op jit(solution)/shard_map/while/body/eval_jaxpr/vmap()/reduce_sum | solution.py:37
  143.9 8.5 %multiply_reduce_fusion.12 = (f32[64,3,128]{2,1,0:T(4,128)S(1)}, f32[64,3,128]{2,1,0:T(4,128)S(1)}) fusion(f32[64,128,128]{2,1,0:T(8,128)S(1)} %get-tuple-element.365, f32[64,128,128]{2,1,0:T(8,128)S(1)} %add_sqrt_fusion.5, f32[64,3,128]{2,1,0:T(4,128)S(1)} %get-tuple-element.356, f32[64,3,128]{2,1,0:T(4,128)S(1)} %get-tuple-element.357), kind=kLoop, calls=%fused_computation.44.clone.1 | loop fusion | flops 15679488 | bytes 8781824 | tf_op jit(solution)/shard_map/while/body/eval_jaxpr/vmap()/reduce_sum | solution.py:37
  172.6 9.2 %subtract_reduce_fusion.2 = (f32[64,128]{1,0:T(8,128)S(1)}, f32[64,128]{1,0:T(8,128)S(1)}, f32[64,128,128]{2,1,0:T(8,128)S(1)}) fusion(f32[64,128,128]{2,1,0:T(8,128)S(1)} %multiply_reduce_fusion.11, f32[64,128]{1,0:T(8,128)S(1)} %bitcast.118, f32[64,128]{1,0:T(8,128)S(1)} %bitcast.115, f32[64,128,128]{2,1,0:T(8,128)S(1)} %fusion.72, ...), kind=kLoop, calls=%fused_computation.59.clone.1 | loop fusion | flops 38780928 | bytes 12845056 | tf_op jit(solution)/shard_map/while/body/eval_jaxpr/vmap()/reduce_sum | solution.py:37
  181.8 8.5 %multiply_reduce_fusion.12 = (f32[64,3,128]{2,1,0:T(4,128)S(1)}, f32[64,3,128]{2,1,0:T(4,128)S(1)}) fusion(f32[64,128,128]{2,1,0:T(8,128)S(1)} %get-tuple-element.365, f32[64,128,128]{2,1,0:T(8,128)S(1)} %add_sqrt_fusion.5, f32[64,3,128]{2,1,0:T(4,128)S(1)} %get-tuple-element.356, f32[64,3,128]{2,1,0:T(4,128)S(1)} %get-tuple-element.357), kind=kLoop, calls=%fused_computation.44.clone.1 | loop fusion | flops 15679488 | bytes 8781824 | tf_op jit(solution)/shard_map/while/body/eval_jaxpr/vmap()/reduce_sum | solution.py:37
  202.3 8.0 multiply_reduce_fusion.11
  210.4 9.2 %subtract_reduce_fusion.2 = (f32[64,128]{1,0:T(8,128)S(1)}, f32[64,128]{1,0:T(8,128)S(1)}, f32[64,128,128]{2,1,0:T(8,128)S(1)}) fusion(f32[64,128,128]{2,1,0:T(8,128)S(1)} %multiply_reduce_fusion.11, f32[64,128]{1,0:T(8,128)S(1)} %bitcast.118, f32[64,128]{1,0:T(8,128)S(1)} %bitcast.115, f32[64,128,128]{2,1,0:T(8,128)S(1)} %fusion.72, ...), kind=kLoop, calls=%fused_computation.59.clone.1 | loop fusion | flops 38780928 | bytes 12845056 | tf_op jit(solution)/shard_map/while/body/eval_jaxpr/vmap()/reduce_sum | solution.py:37
  219.7 8.5 %multiply_reduce_fusion.12 = (f32[64,3,128]{2,1,0:T(4,128)S(1)}, f32[64,3,128]{2,1,0:T(4,128)S(1)}) fusion(f32[64,128,128]{2,1,0:T(8,128)S(1)} %get-tuple-element.365, f32[64,128,128]{2,1,0:T(8,128)S(1)} %add_sqrt_fusion.5, f32[64,3,128]{2,1,0:T(4,128)S(1)} %get-tuple-element.356, f32[64,3,128]{2,1,0:T(4,128)S(1)} %get-tuple-element.357), kind=kLoop, calls=%fused_computation.44.clone.1 | loop fusion | flops 15679488 | bytes 8781824 | tf_op jit(solution)/shard_map/while/body/eval_jaxpr/vmap()/reduce_sum | solution.py:37
  240.2 8.0 multiply_reduce_fusion.11
  248.3 9.2 %subtract_reduce_fusion.2 = (f32[64,128]{1,0:T(8,128)S(1)}, f32[64,128]{1,0:T(8,128)S(1)}, f32[64,128,128]{2,1,0:T(8,128)S(1)}) fusion(f32[64,128,128]{2,1,0:T(8,128)S(1)} %multiply_reduce_fusion.11, f32[64,128]{1,0:T(8,128)S(1)} %bitcast.118, f32[64,128]{1,0:T(8,128)S(1)} %bitcast.115, f32[64,128,128]{2,1,0:T(8,128)S(1)} %fusion.72, ...), kind=kLoop, calls=%fused_computation.59.clone.1 | loop fusion | flops 38780928 | bytes 12845056 | tf_op jit(solution)/shard_map/while/body/eval_jaxpr/vmap()/reduce_sum | solution.py:37
  257.5 8.5 %multiply_reduce_fusion.12 = (f32[64,3,128]{2,1,0:T(4,128)S(1)}, f32[64,3,128]{2,1,0:T(4,128)S(1)}) fusion(f32[64,128,128]{2,1,0:T(8,128)S(1)} %get-tuple-element.365, f32[64,128,128]{2,1,0:T(8,128)S(1)} %add_sqrt_fusion.5, f32[64,3,128]{2,1,0:T(4,128)S(1)} %get-tuple-element.356, f32[64,3,128]{2,1,0:T(4,128)S(1)} %get-tuple-element.357), kind=kLoop, calls=%fused_computation.44.clone.1 | loop fusion | flops 15679488 | bytes 8781824 | tf_op jit(solution)/shard_map/while/body/eval_jaxpr/vmap()/reduce_sum | solution.py:37
  278.0 8.0 multiply_reduce_fusion.11
  286.2 9.2 %subtract_reduce_fusion.2 = (f32[64,128]{1,0:T(8,128)S(1)}, f32[64,128]{1,0:T(8,128)S(1)}, f32[64,128,128]{2,1,0:T(8,128)S(1)}) fusion(f32[64,128,128]{2,1,0:T(8,128)S(1)} %multiply_reduce_fusion.11, f32[64,128]{1,0:T(8,128)S(1)} %bitcast.118, f32[64,128]{1,0:T(8,128)S(1)} %bitcast.115, f32[64,128,128]{2,1,0:T(8,128)S(1)} %fusion.72, ...), kind=kLoop, calls=%fused_computation.59.clone.1 | loop fusion | flops 38780928 | bytes 12845056 | tf_op jit(solution)/shard_map/while/body/eval_jaxpr/vmap()/reduce_sum | solution.py:37
  295.4 8.5 %multiply_reduce_fusion.12 = (f32[64,3,128]{2,1,0:T(4,128)S(1)}, f32[64,3,128]{2,1,0:T(4,128)S(1)}) fusion(f32[64,128,128]{2,1,0:T(8,128)S(1)} %get-tuple-element.365, f32[64,128,128]{2,1,0:T(8,128)S(1)} %add_sqrt_fusion.5, f32[64,3,128]{2,1,0:T(4,128)S(1)} %get-tuple-element.356, f32[64,3,128]{2,1,0:T(4,128)S(1)} %get-tuple-element.357), kind=kLoop, calls=%fused_computation.44.clone.1 | loop fusion | flops 15679488 | bytes 8781824 | tf_op jit(solution)/shard_map/while/body/eval_jaxpr/vmap()/reduce_sum | solution.py:37
  315.9 8.0 multiply_reduce_fusion.11
  324.1 9.2 %subtract_reduce_fusion.2 = (f32[64,128]{1,0:T(8,128)S(1)}, f32[64,128]{1,0:T(8,128)S(1)}, f32[64,128,128]{2,1,0:T(8,128)S(1)}) fusion(f32[64,128,128]{2,1,0:T(8,128)S(1)} %multiply_reduce_fusion.11, f32[64,128]{1,0:T(8,128)S(1)} %bitcast.118, f32[64,128]{1,0:T(8,128)S(1)} %bitcast.115, f32[64,128,128]{2,1,0:T(8,128)S(1)} %fusion.72, ...), kind=kLoop, calls=%fused_computation.59.clone.1 | loop fusion | flops 38780928 | bytes 12845056 | tf_op jit(solution)/shard_map/while/body/eval_jaxpr/vmap()/reduce_sum | solution.py:37
  333.3 8.5 %multiply_reduce_fusion.12 = (f32[64,3,128]{2,1,0:T(4,128)S(1)}, f32[64,3,128]{2,1,0:T(4,128)S(1)}) fusion(f32[64,128,128]{2,1,0:T(8,128)S(1)} %get-tuple-element.365, f32[64,128,128]{2,1,0:T(8,128)S(1)} %add_sqrt_fusion.5, f32[64,3,128]{2,1,0:T(4,128)S(1)} %get-tuple-element.356, f32[64,3,128]{2,1,0:T(4,128)S(1)} %get-tuple-element.357), kind=kLoop, calls=%fused_computation.44.clone.1 | loop fusion | flops 15679488 | bytes 8781824 | tf_op jit(solution)/shard_map/while/body/eval_jaxpr/vmap()/reduce_sum | solution.py:37
  353.8 8.0 multiply_reduce_fusion.11
  362.0 9.2 %subtract_reduce_fusion.2 = (f32[64,128]{1,0:T(8,128)S(1)}, f32[64,128]{1,0:T(8,128)S(1)}, f32[64,128,128]{2,1,0:T(8,128)S(1)}) fusion(f32[64,128,128]{2,1,0:T(8,128)S(1)} %multiply_reduce_fusion.11, f32[64,128]{1,0:T(8,128)S(1)} %bitcast.118, f32[64,128]{1,0:T(8,128)S(1)} %bitcast.115, f32[64,128,128]{2,1,0:T(8,128)S(1)} %fusion.72, ...), kind=kLoop, calls=%fused_computation.59.clone.1 | loop fusion | flops 38780928 | bytes 12845056 | tf_op jit(solution)/shard_map/while/body/eval_jaxpr/vmap()/reduce_sum | solution.py:37
  371.2 8.5 %multiply_reduce_fusion.12 = (f32[64,3,128]{2,1,0:T(4,128)S(1)}, f32[64,3,128]{2,1,0:T(4,128)S(1)}) fusion(f32[64,128,128]{2,1,0:T(8,128)S(1)} %get-tuple-element.365, f32[64,128,128]{2,1,0:T(8,128)S(1)} %add_sqrt_fusion.5, f32[64,3,128]{2,1,0:T(4,128)S(1)} %get-tuple-element.356, f32[64,3,128]{2,1,0:T(4,128)S(1)} %get-tuple-element.357), kind=kLoop, calls=%fused_computation.44.clone.1 | loop fusion | flops 15679488 | bytes 8781824 | tf_op jit(solution)/shard_map/while/body/eval_jaxpr/vmap()/reduce_sum | solution.py:37
  391.7 8.0 multiply_reduce_fusion.11
  399.9 9.2 %subtract_reduce_fusion.2 = (f32[64,128]{1,0:T(8,128)S(1)}, f32[64,128]{1,0:T(8,128)S(1)}, f32[64,128,128]{2,1,0:T(8,128)S(1)}) fusion(f32[64,128,128]{2,1,0:T(8,128)S(1)} %multiply_reduce_fusion.11, f32[64,128]{1,0:T(8,128)S(1)} %bitcast.118, f32[64,128]{1,0:T(8,128)S(1)} %bitcast.115, f32[64,128,128]{2,1,0:T(8,128)S(1)} %fusion.72, ...), kind=kLoop, calls=%fused_computation.59.clone.1 | loop fusion | flops 38780928 | bytes 12845056 | tf_op jit(solution)/shard_map/while/body/eval_jaxpr/vmap()/reduce_sum | solution.py:37
  409.1 8.5 %multiply_reduce_fusion.12 = (f32[64,3,128]{2,1,0:T(4,128)S(1)}, f32[64,3,128]{2,1,0:T(4,128)S(1)}) fusion(f32[64,128,128]{2,1,0:T(8,128)S(1)} %get-tuple-element.365, f32[64,128,128]{2,1,0:T(8,128)S(1)} %add_sqrt_fusion.5, f32[64,3,128]{2,1,0:T(4,128)S(1)} %get-tuple-element.356, f32[64,3,128]{2,1,0:T(4,128)S(1)} %get-tuple-element.357), kind=kLoop, calls=%fused_computation.44.clone.1 | loop fusion | flops 15679488 | bytes 8781824 | tf_op jit(solution)/shard_map/while/body/eval_jaxpr/vmap()/reduce_sum | solution.py:37
  437.7 9.2 %subtract_reduce_fusion.2 = (f32[64,128]{1,0:T(8,128)S(1)}, f32[64,128]{1,0:T(8,128)S(1)}, f32[64,128,128]{2,1,0:T(8,128)S(1)}) fusion(f32[64,128,128]{2,1,0:T(8,128)S(1)} %multiply_reduce_fusion.11, f32[64,128]{1,0:T(8,128)S(1)} %bitcast.118, f32[64,128]{1,0:T(8,128)S(1)} %bitcast.115, f32[64,128,128]{2,1,0:T(8,128)S(1)} %fusion.72, ...), kind=kLoop, calls=%fused_computation.59.clone.1 | loop fusion | flops 38780928 | bytes 12845056 | tf_op jit(solution)/shard_map/while/body/eval_jaxpr/vmap()/reduce_sum | solution.py:37
  446.9 8.5 %multiply_reduce_fusion.12 = (f32[64,3,128]{2,1,0:T(4,128)S(1)}, f32[64,3,128]{2,1,0:T(4,128)S(1)}) fusion(f32[64,128,128]{2,1,0:T(8,128)S(1)} %get-tuple-element.365, f32[64,128,128]{2,1,0:T(8,128)S(1)} %add_sqrt_fusion.5, f32[64,3,128]{2,1,0:T(4,128)S(1)} %get-tuple-element.356, f32[64,3,128]{2,1,0:T(4,128)S(1)} %get-tuple-element.357), kind=kLoop, calls=%fused_computation.44.clone.1 | loop fusion | flops 15679488 | bytes 8781824 | tf_op jit(solution)/shard_map/while/body/eval_jaxpr/vmap()/reduce_sum | solution.py:37
  467.4 8.0 multiply_reduce_fusion.11
  475.6 9.2 %subtract_reduce_fusion.2 = (f32[64,128]{1,0:T(8,128)S(1)}, f32[64,128]{1,0:T(8,128)S(1)}, f32[64,128,128]{2,1,0:T(8,128)S(1)}) fusion(f32[64,128,128]{2,1,0:T(8,128)S(1)} %multiply_reduce_fusion.11, f32[64,128]{1,0:T(8,128)S(1)} %bitcast.118, f32[64,128]{1,0:T(8,128)S(1)} %bitcast.115, f32[64,128,128]{2,1,0:T(8,128)S(1)} %fusion.72, ...), kind=kLoop, calls=%fused_computation.59.clone.1 | loop fusion | flops 38780928 | bytes 12845056 | tf_op jit(solution)/shard_map/while/body/eval_jaxpr/vmap()/reduce_sum | solution.py:37
  484.8 8.5 %multiply_reduce_fusion.12 = (f32[64,3,128]{2,1,0:T(4,128)S(1)}, f32[64,3,128]{2,1,0:T(4,128)S(1)}) fusion(f32[64,128,128]{2,1,0:T(8,128)S(1)} %get-tuple-element.365, f32[64,128,128]{2,1,0:T(8,128)S(1)} %add_sqrt_fusion.5, f32[64,3,128]{2,1,0:T(4,128)S(1)} %get-tuple-element.356, f32[64,3,128]{2,1,0:T(4,128)S(1)} %get-tuple-element.357), kind=kLoop, calls=%fused_computation.44.clone.1 | loop fusion | flops 15679488 | bytes 8781824 | tf_op jit(solution)/shard_map/while/body/eval_jaxpr/vmap()/reduce_sum | solution.py:37
  505.3 8.0 multiply_reduce_fusion.11
  513.5 9.2 %subtract_reduce_fusion.2 = (f32[64,128]{1,0:T(8,128)S(1)}, f32[64,128]{1,0:T(8,128)S(1)}, f32[64,128,128]{2,1,0:T(8,128)S(1)}) fusion(f32[64,128,128]{2,1,0:T(8,128)S(1)} %multiply_reduce_fusion.11, f32[64,128]{1,0:T(8,128)S(1)} %bitcast.118, f32[64,128]{1,0:T(8,128)S(1)} %bitcast.115, f32[64,128,128]{2,1,0:T(8,128)S(1)} %fusion.72, ...), kind=kLoop, calls=%fused_computation.59.clone.1 | loop fusion | flops 38780928 | bytes 12845056 | tf_op jit(solution)/shard_map/while/body/eval_jaxpr/vmap()/reduce_sum | solution.py:37
  522.7 8.5 %multiply_reduce_fusion.12 = (f32[64,3,128]{2,1,0:T(4,128)S(1)}, f32[64,3,128]{2,1,0:T(4,128)S(1)}) fusion(f32[64,128,128]{2,1,0:T(8,128)S(1)} %get-tuple-element.365, f32[64,128,128]{2,1,0:T(8,128)S(1)} %add_sqrt_fusion.5, f32[64,3,128]{2,1,0:T(4,128)S(1)} %get-tuple-element.356, f32[64,3,128]{2,1,0:T(4,128)S(1)} %get-tuple-element.357), kind=kLoop, calls=%fused_computation.44.clone.1 | loop fusion | flops 15679488 | bytes 8781824 | tf_op jit(solution)/shard_map/while/body/eval_jaxpr/vmap()/reduce_sum | solution.py:37
  551.4 9.2 %subtract_reduce_fusion.2 = (f32[64,128]{1,0:T(8,128)S(1)}, f32[64,128]{1,0:T(8,128)S(1)}, f32[64,128,128]{2,1,0:T(8,128)S(1)}) fusion(f32[64,128,128]{2,1,0:T(8,128)S(1)} %multiply_reduce_fusion.11, f32[64,128]{1,0:T(8,128)S(1)} %bitcast.118, f32[64,128]{1,0:T(8,128)S(1)} %bitcast.115, f32[64,128,128]{2,1,0:T(8,128)S(1)} %fusion.72, ...), kind=kLoop, calls=%fused_computation.59.clone.1 | loop fusion | flops 38780928 | bytes 12845056 | tf_op jit(solution)/shard_map/while/body/eval_jaxpr/vmap()/reduce_sum | solution.py:37
  560.6 8.5 %multiply_reduce_fusion.12 = (f32[64,3,128]{2,1,0:T(4,128)S(1)}, f32[64,3,128]{2,1,0:T(4,128)S(1)}) fusion(f32[64,128,128]{2,1,0:T(8,128)S(1)} %get-tuple-element.365, f32[64,128,128]{2,1,0:T(8,128)S(1)} %add_sqrt_fusion.5, f32[64,3,128]{2,1,0:T(4,128)S(1)} %get-tuple-element.356, f32[64,3,128]{2,1,0:T(4,128)S(1)} %get-tuple-element.357), kind=kLoop, calls=%fused_computation.44.clone.1 | loop fusion | flops 15679488 | bytes 8781824 | tf_op jit(solution)/shard_map/while/body/eval_jaxpr/vmap()/reduce_sum | solution.py:37
  589.2 9.2 %subtract_reduce_fusion.2 = (f32[64,128]{1,0:T(8,128)S(1)}, f32[64,128]{1,0:T(8,128)S(1)}, f32[64,128,128]{2,1,0:T(8,128)S(1)}) fusion(f32[64,128,128]{2,1,0:T(8,128)S(1)} %multiply_reduce_fusion.11, f32[64,128]{1,0:T(8,128)S(1)} %bitcast.118, f32[64,128]{1,0:T(8,128)S(1)} %bitcast.115, f32[64,128,128]{2,1,0:T(8,128)S(1)} %fusion.72, ...), kind=kLoop, calls=%fused_computation.59.clone.1 | loop fusion | flops 38780928 | bytes 12845056 | tf_op jit(solution)/shard_map/while/body/eval_jaxpr/vmap()/reduce_sum | solution.py:37
  598.4 8.5 %multiply_reduce_fusion.12 = (f32[64,3,128]{2,1,0:T(4,128)S(1)}, f32[64,3,128]{2,1,0:T(4,128)S(1)}) fusion(f32[64,128,128]{2,1,0:T(8,128)S(1)} %get-tuple-element.365, f32[64,128,128]{2,1,0:T(8,128)S(1)} %add_sqrt_fusion.5, f32[64,3,128]{2,1,0:T(4,128)S(1)} %get-tuple-element.356, f32[64,3,128]{2,1,0:T(4,128)S(1)} %get-tuple-element.357), kind=kLoop, calls=%fused_computation.44.clone.1 | loop fusion | flops 15679488 | bytes 8781824 | tf_op jit(solution)/shard_map/while/body/eval_jaxpr/vmap()/reduce_sum | solution.py:37
  627.1 9.2 %subtract_reduce_fusion.2 = (f32[64,128]{1,0:T(8,128)S(1)}, f32[64,128]{1,0:T(8,128)S(1)}, f32[64,128,128]{2,1,0:T(8,128)S(1)}) fusion(f32[64,128,128]{2,1,0:T(8,128)S(1)} %multiply_reduce_fusion.11, f32[64,128]{1,0:T(8,128)S(1)} %bitcast.118, f32[64,128]{1,0:T(8,128)S(1)} %bitcast.115, f32[64,128,128]{2,1,0:T(8,128)S(1)} %fusion.72, ...), kind=kLoop, calls=%fused_computation.59.clone.1 | loop fusion | flops 38780928 | bytes 12845056 | tf_op jit(solution)/shard_map/while/body/eval_jaxpr/vmap()/reduce_sum | solution.py:37
  636.3 8.5 %multiply_reduce_fusion.12 = (f32[64,3,128]{2,1,0:T(4,128)S(1)}, f32[64,3,128]{2,1,0:T(4,128)S(1)}) fusion(f32[64,128,128]{2,1,0:T(8,128)S(1)} %get-tuple-element.365, f32[64,128,128]{2,1,0:T(8,128)S(1)} %add_sqrt_fusion.5, f32[64,3,128]{2,1,0:T(4,128)S(1)} %get-tuple-element.356, f32[64,3,128]{2,1,0:T(4,128)S(1)} %get-tuple-element.357), kind=kLoop, calls=%fused_computation.44.clone.1 | loop fusion | flops 15679488 | bytes 8781824 | tf_op jit(solution)/shard_map/while/body/eval_jaxpr/vmap()/reduce_sum | solution.py:37
  665.0 9.2 %subtract_reduce_fusion.2 = (f32[64,128]{1,0:T(8,128)S(1)}, f32[64,128]{1,0:T(8,128)S(1)}, f32[64,128,128]{2,1,0:T(8,128)S(1)}) fusion(f32[64,128,128]{2,1,0:T(8,128)S(1)} %multiply_reduce_fusion.11, f32[64,128]{1,0:T(8,128)S(1)} %bitcast.118, f32[64,128]{1,0:T(8,128)S(1)} %bitcast.115, f32[64,128,128]{2,1,0:T(8,128)S(1)} %fusion.72, ...), kind=kLoop, calls=%fused_computation.59.clone.1 | loop fusion | flops 38780928 | bytes 12845056 | tf_op jit(solution)/shard_map/while/body/eval_jaxpr/vmap()/reduce_sum | solution.py:37
  674.2 8.5 %multiply_reduce_fusion.12 = (f32[64,3,128]{2,1,0:T(4,128)S(1)}, f32[64,3,128]{2,1,0:T(4,128)S(1)}) fusion(f32[64,128,128]{2,1,0:T(8,128)S(1)} %get-tuple-element.365, f32[64,128,128]{2,1,0:T(8,128)S(1)} %add_sqrt_fusion.5, f32[64,3,128]{2,1,0:T(4,128)S(1)} %get-tuple-element.356, f32[64,3,128]{2,1,0:T(4,128)S(1)} %get-tuple-element.357), kind=kLoop, calls=%fused_computation.44.clone.1 | loop fusion | flops 15679488 | bytes 8781824 | tf_op jit(solution)/shard_map/while/body/eval_jaxpr/vmap()/reduce_sum | solution.py:37
  702.9 9.2 %subtract_reduce_fusion.2 = (f32[64,128]{1,0:T(8,128)S(1)}, f32[64,128]{1,0:T(8,128)S(1)}, f32[64,128,128]{2,1,0:T(8,128)S(1)}) fusion(f32[64,128,128]{2,1,0:T(8,128)S(1)} %multiply_reduce_fusion.11, f32[64,128]{1,0:T(8,128)S(1)} %bitcast.118, f32[64,128]{1,0:T(8,128)S(1)} %bitcast.115, f32[64,128,128]{2,1,0:T(8,128)S(1)} %fusion.72, ...), kind=kLoop, calls=%fused_computation.59.clone.1 | loop fusion | flops 38780928 | bytes 12845056 | tf_op jit(solution)/shard_map/while/body/eval_jaxpr/vmap()/reduce_sum | solution.py:37
  712.1 8.5 %multiply_reduce_fusion.12 = (f32[64,3,128]{2,1,0:T(4,128)S(1)}, f32[64,3,128]{2,1,0:T(4,128)S(1)}) fusion(f32[64,128,128]{2,1,0:T(8,128)S(1)} %get-tuple-element.365, f32[64,128,128]{2,1,0:T(8,128)S(1)} %add_sqrt_fusion.5, f32[64,3,128]{2,1,0:T(4,128)S(1)} %get-tuple-element.356, f32[64,3,128]{2,1,0:T(4,128)S(1)} %get-tuple-element.357), kind=kLoop, calls=%fused_computation.44.clone.1 | loop fusion | flops 15679488 | bytes 8781824 | tf_op jit(solution)/shard_map/while/body/eval_jaxpr/vmap()/reduce_sum | solution.py:37
  725.8 10.5 %collective-permute-done.1 = f32[192,512]{1,0:T(8,128)S(1)} collective-permute-done((f32[192,512]{1,0:T(8,128)S(1)}, f32[192,512]{1,0:T(8,128)S(1)}, u32[]{:S(2)}, u32[]{:S(2)}) %collective-permute-start.1) | collective-permute-done | bytes 393248 | tf_op jit(solution)/shard_map/ppermute | solution.py:15
  741.3 69.2 %while.27 = (s32[]{:T(128)}, f32[8,16,4,128]{3,2,1,0:T(4,128)S(1)}, f32[8,16,9,128]{3,1,0,2:T(8,128)}, s32[]{:T(128)}) while((s32[]{:T(128)}, f32[8,16,4,128]{3,2,1,0:T(4,128)S(1)}, f32[8,16,9,128]{3,1,0,2:T(8,128)}, s32[]{:T(128)}) %tuple.104), condition=%wide.region_14.15_spmd, body=%wide.region_9.14_spmd.sunk | while | flops 18925568 | bytes 11239485 | solution.py:146
  810.5 14.3 %reduce-scatter.2.cloned.1.call-done = f32[128,512]{1,0:T(8,128)} async-done(((f32[2048,512]{1,0:T(8,128)}), f32[128,512]{1,0:T(8,128)}) %reduce-scatter.2.cloned.1.call-update) | async-done | bytes 262160 | tf_op jit(solution)/shard_map/reduce_scatter | solution.py:135
  (658 shorter events, 347.6 us)
Async XLA Ops:
  6.5 83.9 %all-gather.2.cloned.1.call-start = ((), (), s32[]{:S(2)}) async-start(), calls=%async_computation.1 | async-start | bytes 10027008 | tf_op jit(solution)/shard_map/all_gather | solution.py:95
  11.8 813.0 %reduce-scatter.2.cloned.1.call-start = ((), (), s32[]{:S(2)}) async-start(), calls=%async_computation.2 | async-start | bytes 4456448 | tf_op jit(solution)/shard_map/reduce_scatter | solution.py:135
  103.2 9.5 %copy-start.8 = (s32[1,1024,2]{1,2,0:T(2,128)S(1)}, s32[1,1024,2]{1,2,0:T(2,128)}, u32[]{:S(2)}) copy-start(s32[1,1024,2]{1,2,0:T(2,128)} %param.18) | copy-start | bytes 24580
  110.9 4.0 collective-permute-start
  143.9 8.6 %copy-start.5 = (s32[16,64]{1,0:T(8,128)S(1)}, s32[16,64]{1,0:T(8,128)}, u32[]{:S(2)}) copy-start(s32[16,64]{1,0:T(8,128)} %copy-done.4) | copy-start | bytes 12292 | tf_op jit(solution)/shard_map/while
  143.9 8.6 %copy-start.7 = (s32[16,64]{1,0:T(8,128)S(1)}, s32[16,64]{1,0:T(8,128)}, u32[]{:S(2)}) copy-start(s32[16,64]{1,0:T(8,128)} %copy-done.6) | copy-start | bytes 12292 | tf_op jit(solution)/shard_map/while
  143.9 10.1 %copy-start = (f32[192,512]{1,0:T(8,128)S(1)}, f32[192,512]{1,0:T(8,128)}, u32[]{:S(2)}) copy-start(f32[192,512]{1,0:T(8,128)} %get-tuple-element.382) | copy-start | bytes 1179652 | tf_op jit(solution)/shard_map/while
  181.7 8.6 %copy-start.5 = (s32[16,64]{1,0:T(8,128)S(1)}, s32[16,64]{1,0:T(8,128)}, u32[]{:S(2)}) copy-start(s32[16,64]{1,0:T(8,128)} %copy-done.4) | copy-start | bytes 12292 | tf_op jit(solution)/shard_map/while
  181.8 8.6 %copy-start.7 = (s32[16,64]{1,0:T(8,128)S(1)}, s32[16,64]{1,0:T(8,128)}, u32[]{:S(2)}) copy-start(s32[16,64]{1,0:T(8,128)} %copy-done.6) | copy-start | bytes 12292 | tf_op jit(solution)/shard_map/while
  181.8 10.1 %copy-start = (f32[192,512]{1,0:T(8,128)S(1)}, f32[192,512]{1,0:T(8,128)}, u32[]{:S(2)}) copy-start(f32[192,512]{1,0:T(8,128)} %get-tuple-element.382) | copy-start | bytes 1179652 | tf_op jit(solution)/shard_map/while
  219.6 8.6 %copy-start.5 = (s32[16,64]{1,0:T(8,128)S(1)}, s32[16,64]{1,0:T(8,128)}, u32[]{:S(2)}) copy-start(s32[16,64]{1,0:T(8,128)} %copy-done.4) | copy-start | bytes 12292 | tf_op jit(solution)/shard_map/while
  219.6 8.6 %copy-start.7 = (s32[16,64]{1,0:T(8,128)S(1)}, s32[16,64]{1,0:T(8,128)}, u32[]{:S(2)}) copy-start(s32[16,64]{1,0:T(8,128)} %copy-done.6) | copy-start | bytes 12292 | tf_op jit(solution)/shard_map/while
  219.6 10.1 %copy-start = (f32[192,512]{1,0:T(8,128)S(1)}, f32[192,512]{1,0:T(8,128)}, u32[]{:S(2)}) copy-start(f32[192,512]{1,0:T(8,128)} %get-tuple-element.382) | copy-start | bytes 1179652 | tf_op jit(solution)/shard_map/while
  257.5 8.6 %copy-start.5 = (s32[16,64]{1,0:T(8,128)S(1)}, s32[16,64]{1,0:T(8,128)}, u32[]{:S(2)}) copy-start(s32[16,64]{1,0:T(8,128)} %copy-done.4) | copy-start | bytes 12292 | tf_op jit(solution)/shard_map/while
  257.5 8.6 %copy-start.7 = (s32[16,64]{1,0:T(8,128)S(1)}, s32[16,64]{1,0:T(8,128)}, u32[]{:S(2)}) copy-start(s32[16,64]{1,0:T(8,128)} %copy-done.6) | copy-start | bytes 12292 | tf_op jit(solution)/shard_map/while
  257.5 10.1 %copy-start = (f32[192,512]{1,0:T(8,128)S(1)}, f32[192,512]{1,0:T(8,128)}, u32[]{:S(2)}) copy-start(f32[192,512]{1,0:T(8,128)} %get-tuple-element.382) | copy-start | bytes 1179652 | tf_op jit(solution)/shard_map/while
  295.4 8.6 %copy-start.5 = (s32[16,64]{1,0:T(8,128)S(1)}, s32[16,64]{1,0:T(8,128)}, u32[]{:S(2)}) copy-start(s32[16,64]{1,0:T(8,128)} %copy-done.4) | copy-start | bytes 12292 | tf_op jit(solution)/shard_map/while
  295.4 8.6 %copy-start.7 = (s32[16,64]{1,0:T(8,128)S(1)}, s32[16,64]{1,0:T(8,128)}, u32[]{:S(2)}) copy-start(s32[16,64]{1,0:T(8,128)} %copy-done.6) | copy-start | bytes 12292 | tf_op jit(solution)/shard_map/while
  295.4 10.1 %copy-start = (f32[192,512]{1,0:T(8,128)S(1)}, f32[192,512]{1,0:T(8,128)}, u32[]{:S(2)}) copy-start(f32[192,512]{1,0:T(8,128)} %get-tuple-element.382) | copy-start | bytes 1179652 | tf_op jit(solution)/shard_map/while
  333.3 8.6 %copy-start.5 = (s32[16,64]{1,0:T(8,128)S(1)}, s32[16,64]{1,0:T(8,128)}, u32[]{:S(2)}) copy-start(s32[16,64]{1,0:T(8,128)} %copy-done.4) | copy-start | bytes 12292 | tf_op jit(solution)/shard_map/while
  333.3 8.6 %copy-start.7 = (s32[16,64]{1,0:T(8,128)S(1)}, s32[16,64]{1,0:T(8,128)}, u32[]{:S(2)}) copy-start(s32[16,64]{1,0:T(8,128)} %copy-done.6) | copy-start | bytes 12292 | tf_op jit(solution)/shard_map/while
  333.3 10.1 %copy-start = (f32[192,512]{1,0:T(8,128)S(1)}, f32[192,512]{1,0:T(8,128)}, u32[]{:S(2)}) copy-start(f32[192,512]{1,0:T(8,128)} %get-tuple-element.382) | copy-start | bytes 1179652 | tf_op jit(solution)/shard_map/while
  371.1 8.6 %copy-start.5 = (s32[16,64]{1,0:T(8,128)S(1)}, s32[16,64]{1,0:T(8,128)}, u32[]{:S(2)}) copy-start(s32[16,64]{1,0:T(8,128)} %copy-done.4) | copy-start | bytes 12292 | tf_op jit(solution)/shard_map/while
  371.2 8.6 %copy-start.7 = (s32[16,64]{1,0:T(8,128)S(1)}, s32[16,64]{1,0:T(8,128)}, u32[]{:S(2)}) copy-start(s32[16,64]{1,0:T(8,128)} %copy-done.6) | copy-start | bytes 12292 | tf_op jit(solution)/shard_map/while
  371.2 10.1 %copy-start = (f32[192,512]{1,0:T(8,128)S(1)}, f32[192,512]{1,0:T(8,128)}, u32[]{:S(2)}) copy-start(f32[192,512]{1,0:T(8,128)} %get-tuple-element.382) | copy-start | bytes 1179652 | tf_op jit(solution)/shard_map/while
  409.0 8.6 %copy-start.5 = (s32[16,64]{1,0:T(8,128)S(1)}, s32[16,64]{1,0:T(8,128)}, u32[]{:S(2)}) copy-start(s32[16,64]{1,0:T(8,128)} %copy-done.4) | copy-start | bytes 12292 | tf_op jit(solution)/shard_map/while
  409.0 8.6 %copy-start.7 = (s32[16,64]{1,0:T(8,128)S(1)}, s32[16,64]{1,0:T(8,128)}, u32[]{:S(2)}) copy-start(s32[16,64]{1,0:T(8,128)} %copy-done.6) | copy-start | bytes 12292 | tf_op jit(solution)/shard_map/while
  409.0 10.1 %copy-start = (f32[192,512]{1,0:T(8,128)S(1)}, f32[192,512]{1,0:T(8,128)}, u32[]{:S(2)}) copy-start(f32[192,512]{1,0:T(8,128)} %get-tuple-element.382) | copy-start | bytes 1179652 | tf_op jit(solution)/shard_map/while
  446.9 8.6 %copy-start.5 = (s32[16,64]{1,0:T(8,128)S(1)}, s32[16,64]{1,0:T(8,128)}, u32[]{:S(2)}) copy-start(s32[16,64]{1,0:T(8,128)} %copy-done.4) | copy-start | bytes 12292 | tf_op jit(solution)/shard_map/while
  446.9 8.6 %copy-start.7 = (s32[16,64]{1,0:T(8,128)S(1)}, s32[16,64]{1,0:T(8,128)}, u32[]{:S(2)}) copy-start(s32[16,64]{1,0:T(8,128)} %copy-done.6) | copy-start | bytes 12292 | tf_op jit(solution)/shard_map/while
  446.9 10.1 %copy-start = (f32[192,512]{1,0:T(8,128)S(1)}, f32[192,512]{1,0:T(8,128)}, u32[]{:S(2)}) copy-start(f32[192,512]{1,0:T(8,128)} %get-tuple-element.382) | copy-start | bytes 1179652 | tf_op jit(solution)/shard_map/while
  484.8 8.6 %copy-start.5 = (s32[16,64]{1,0:T(8,128)S(1)}, s32[16,64]{1,0:T(8,128)}, u32[]{:S(2)}) copy-start(s32[16,64]{1,0:T(8,128)} %copy-done.4) | copy-start | bytes 12292 | tf_op jit(solution)/shard_map/while
  484.8 8.6 %copy-start.7 = (s32[16,64]{1,0:T(8,128)S(1)}, s32[16,64]{1,0:T(8,128)}, u32[]{:S(2)}) copy-start(s32[16,64]{1,0:T(8,128)} %copy-done.6) | copy-start | bytes 12292 | tf_op jit(solution)/shard_map/while
  484.8 10.1 %copy-start = (f32[192,512]{1,0:T(8,128)S(1)}, f32[192,512]{1,0:T(8,128)}, u32[]{:S(2)}) copy-start(f32[192,512]{1,0:T(8,128)} %get-tuple-element.382) | copy-start | bytes 1179652 | tf_op jit(solution)/shard_map/while
  522.7 8.6 %copy-start.5 = (s32[16,64]{1,0:T(8,128)S(1)}, s32[16,64]{1,0:T(8,128)}, u32[]{:S(2)}) copy-start(s32[16,64]{1,0:T(8,128)} %copy-done.4) | copy-start | bytes 12292 | tf_op jit(solution)/shard_map/while
  522.7 8.6 %copy-start.7 = (s32[16,64]{1,0:T(8,128)S(1)}, s32[16,64]{1,0:T(8,128)}, u32[]{:S(2)}) copy-start(s32[16,64]{1,0:T(8,128)} %copy-done.6) | copy-start | bytes 12292 | tf_op jit(solution)/shard_map/while
  522.7 10.1 %copy-start = (f32[192,512]{1,0:T(8,128)S(1)}, f32[192,512]{1,0:T(8,128)}, u32[]{:S(2)}) copy-start(f32[192,512]{1,0:T(8,128)} %get-tuple-element.382) | copy-start | bytes 1179652 | tf_op jit(solution)/shard_map/while
  560.5 8.6 %copy-start.5 = (s32[16,64]{1,0:T(8,128)S(1)}, s32[16,64]{1,0:T(8,128)}, u32[]{:S(2)}) copy-start(s32[16,64]{1,0:T(8,128)} %copy-done.4) | copy-start | bytes 12292 | tf_op jit(solution)/shard_map/while
  560.6 8.6 %copy-start.7 = (s32[16,64]{1,0:T(8,128)S(1)}, s32[16,64]{1,0:T(8,128)}, u32[]{:S(2)}) copy-start(s32[16,64]{1,0:T(8,128)} %copy-done.6) | copy-start | bytes 12292 | tf_op jit(solution)/shard_map/while
  560.6 10.1 %copy-start = (f32[192,512]{1,0:T(8,128)S(1)}, f32[192,512]{1,0:T(8,128)}, u32[]{:S(2)}) copy-start(f32[192,512]{1,0:T(8,128)} %get-tuple-element.382) | copy-start | bytes 1179652 | tf_op jit(solution)/shard_map/while
  598.4 8.6 %copy-start.5 = (s32[16,64]{1,0:T(8,128)S(1)}, s32[16,64]{1,0:T(8,128)}, u32[]{:S(2)}) copy-start(s32[16,64]{1,0:T(8,128)} %copy-done.4) | copy-start | bytes 12292 | tf_op jit(solution)/shard_map/while
  598.4 8.6 %copy-start.7 = (s32[16,64]{1,0:T(8,128)S(1)}, s32[16,64]{1,0:T(8,128)}, u32[]{:S(2)}) copy-start(s32[16,64]{1,0:T(8,128)} %copy-done.6) | copy-start | bytes 12292 | tf_op jit(solution)/shard_map/while
  598.4 10.1 %copy-start = (f32[192,512]{1,0:T(8,128)S(1)}, f32[192,512]{1,0:T(8,128)}, u32[]{:S(2)}) copy-start(f32[192,512]{1,0:T(8,128)} %get-tuple-element.382) | copy-start | bytes 1179652 | tf_op jit(solution)/shard_map/while
  636.3 8.6 %copy-start.5 = (s32[16,64]{1,0:T(8,128)S(1)}, s32[16,64]{1,0:T(8,128)}, u32[]{:S(2)}) copy-start(s32[16,64]{1,0:T(8,128)} %copy-done.4) | copy-start | bytes 12292 | tf_op jit(solution)/shard_map/while
  636.3 10.1 %copy-start = (f32[192,512]{1,0:T(8,128)S(1)}, f32[192,512]{1,0:T(8,128)}, u32[]{:S(2)}) copy-start(f32[192,512]{1,0:T(8,128)} %get-tuple-element.382) | copy-start | bytes 1179652 | tf_op jit(solution)/shard_map/while
  674.2 10.1 %copy-start = (f32[192,512]{1,0:T(8,128)S(1)}, f32[192,512]{1,0:T(8,128)}, u32[]{:S(2)}) copy-start(f32[192,512]{1,0:T(8,128)} %get-tuple-element.382) | copy-start | bytes 1179652 | tf_op jit(solution)/shard_map/while
  712.1 10.1 %copy-start = (f32[192,512]{1,0:T(8,128)S(1)}, f32[192,512]{1,0:T(8,128)}, u32[]{:S(2)}) copy-start(f32[192,512]{1,0:T(8,128)} %get-tuple-element.382) | copy-start | bytes 1179652 | tf_op jit(solution)/shard_map/while
  723.4 12.9 %collective-permute-start.1 = (f32[192,512]{1,0:T(8,128)S(1)}, f32[192,512]{1,0:T(8,128)S(1)}, u32[]{:S(2)}, u32[]{:S(2)}) collective-permute-start(f32[192,512]{1,0:T(8,128)S(1)} %slice.109), channel_id=1, source_target_pairs={{16,0},{32,16},{48,32},{64,48},{80,64},{96,80},{112,96},{17,1},{33... | collective-permute-start | bytes 1179656 | tf_op jit(solution)/shard_map/ppermute | solution.py:15
  (70 other events, 176.8 us)
Sparse Core Ops, SparseCore 0:
  12.0 78.4 all-gather.1
  741.4 83.3 reduce-scatter.1
where the time goes:
time: 836 us; the launch traced here: 833 us
  other arithmetic  564 us (67%)
  local copies, waits for them, and re-layouts  123 us (15%)
  waiting for transfers between devices  76 us (9%)
  blocking collectives  25.4 us (3%)
  matrix products  23.4 us (3%)
  between operations  14.2 us (2%)
    reduce_sum x16, other arithmetic, tile_pair(): jnp.sum(viscous - conduct, 0)[None]  147 us
    reduce_sum x16, other arithmetic, tile_pair(): jnp.sum(force, 1)  135 us
    reduce_sum x16, other arithmetic, tile_pair(): along = jnp.sum(unit * relative, 0)  128 us
    reduce_sum x16, other arithmetic, tile_pair(): radius = jnp.sqrt(jnp.sum(offset * offset, 0) + 0.01)  66.2 us
    all_gather x1, waiting for transfers between devices, per_device(): group_data = lax.all_gather(owned, 'tile', axis=0, tiled=True)  50.3 us
    gather x16, local copies, waits for them, and re-layouts, consume(): reachable[second_index]  39.7 us
    all_gather x1, blocking collectives, per_device(): tables = lax.all_gather(exported_tile_places, 'tile', axis=0, tiled=True)  25.4 us
    mul x8, other arithmetic, tile_self(): (repulse * weight - friction * weight * weight * along + noise_amp * weig...  19.2 us
  transfers between devices with their start and end apart: 4, of which 4 were waited for; matrix products, arithmetic and copies ran while one was open for 9% of the time, Pallas kernels for 0%

commit v1 on v0

--- a/solution.py
+++ b/solution.py
@@ -92,7 +92,9 @@
         0,
     )
     owned = owned.reshape(9, blocks, 128).transpose(1, 0, 2)
-    group_data = lax.all_gather(owned, "tile", axis=0, tiled=True)
+    group_data = jnp.concatenate(
+        lax.all_to_all(jnp.stack([owned] * lax.axis_size("tile")), "tile", 0, 0), axis=0
+    )
     tables = lax.all_gather(exported_tile_places, "tile", axis=0, tiled=True)
     my_index = lax.axis_index("tile")
     my_slots = lax.dynamic_index_in_dim(tables, my_index, 1, keepdims=False)

time: 836 us -> 972 us (1.16)
  blocking collectives: 25.4 us -> 186 us
  waiting for transfers between devices: 76 us -> 25.6 us
  local copies, waits for them, and re-layouts: 123 us -> 141 us
    all_gather x1, blocking collectives: 25.4 us -> 186 us  [per_device(): tables = lax.all_gather(exported_tile_places, 'tile', axis=0, tiled=True)]
    all_gather x1 -> x0, waiting for transfers between devices: 50.3 us -> none  [per_device(): group_data = lax.all_gather(owned, 'tile', axis=0, tiled=True)]
    reshape x0 -> x1, local copies, waits for them, and re-layouts: none -> 22.5 us  [per_device(): jnp.concatenate(lax.all_to_all(jnp.stack([owned] * lax.axis_size('tile'))...]
    all_gather x1 -> x0, local copies, waits for them, and re-layouts: 12.8 us -> none  [per_device(): group_data = lax.all_gather(owned, 'tile', axis=0, tiled=True)]
  transfers between devices with their start and end apart: 4 -> 4, of which waited for: 4 -> 3; matrix products, arithmetic and copies ran while one was open for 9% -> 7% of each run, Pallas kernels for 0% -> 0%
where the time goes in v1:
time: 972 us; the launch traced here: 970 us
  other arithmetic  564 us (58%)
  blocking collectives  186 us (19%)
  local copies, waits for them, and re-layouts  141 us (15%)
  waiting for transfers between devices  25.6 us (3%)
  matrix products  23.4 us (2%)
  between operations  14.2 us (1%)
  starting transfers between devices  11.4 us (1%)
    all_gather x1, blocking collectives, per_device(): tables = lax.all_gather(exported_tile_places, 'tile', axis=0, tiled=True)  186 us
    reduce_sum x16, other arithmetic, tile_pair(): jnp.sum(viscous - conduct, 0)[None]  147 us
    reduce_sum x16, other arithmetic, tile_pair(): jnp.sum(force, 1)  135 us
    reduce_sum x16, other arithmetic, tile_pair(): along = jnp.sum(unit * relative, 0)  128 us
    reduce_sum x16, other arithmetic, tile_pair(): radius = jnp.sqrt(jnp.sum(offset * offset, 0) + 0.01)  66.2 us
    gather x16, local copies, waits for them, and re-layouts, consume(): reachable[second_index]  39.7 us
    reshape x1, local copies, waits for them, and re-layouts, per_device(): jnp.concatenate(lax.all_to_all(jnp.stack([owned] * lax.axis_size('tile'))...  22.5 us
  transfers between devices with their start and end apart: 4, of which 3 were waited for; matrix products, arithmetic and copies ran while one was open for 7% of the time, Pallas kernels for 0%

profile of v1, /device:TPU:0, one launch (start us, length us, event | category | flops | bytes accessed | tf_op | source)
XLA Modules:
  0.0 969.7 jit_solution(10995851649398289915)
XLA Ops:
  16.7 8.3 all-to-all-start
  25.1 185.6 %all_gather.3 = s32[16,16,12]{2,1,0:T(8,128)S(1)} all-gather(s32[1,16,12]{2,1,0:T(8,128)S(1)} %copy.43), channel_id=1, replica_groups=mesh['grp'=8,'tile'=16] {'tile'}, dimensions={0}, use_global_device_ids=true | all-gather | bytes 13056 | tf_op jit(solution)/shard_map/all_gather | solution.py:98
  217.2 22.5 %copy.45 = f32[2048,9,128]{2,1,0:T(8,128)} copy(f32[2048,9,128]{2,0,1:T(8,128)S(1)} %bitcast.110) | data formatting | bytes 18874368 | tf_op jit(solution)/shard_map/reshape | solution.py:95
  253.4 606.1 %while.28 = (s32[]{:T(128)}, f32[192,512]{1,0:T(8,128)}, f32[384,512]{1,0:T(8,128)S(1)}, s32[16,64]{1,0:T(8,128)S(1)}, f32[192,9,128]{2,1,0:T(8,128)S(1)}, /*ind...) while((s32[]{:T(128)}, f32[192,512]{1,0:T(8,128)}, ...), condition=%wide.region_7.8_spmd.clone, body=%wide.region_0.7_spmd.clone.sunk | while | flops 305871232 | bytes 52507452 | solution.py:133
  262.5 8.0 multiply_reduce_fusion.11
  270.7 9.2 subtract_reduce_fusion.2
  279.9 8.5 multiply_reduce_fusion.12
  300.4 8.0 multiply_reduce_fusion.11
  308.6 9.2 subtract_reduce_fusion.2
  317.8 8.5 multiply_reduce_fusion.12
  338.3 8.0 multiply_reduce_fusion.11
  346.5 9.2 subtract_reduce_fusion.2
  355.7 8.5 multiply_reduce_fusion.12
  376.2 8.0 multiply_reduce_fusion.11
  384.4 9.2 subtract_reduce_fusion.2
  393.6 8.5 multiply_reduce_fusion.12
  414.1 8.0 multiply_reduce_fusion.11
  422.2 9.2 subtract_reduce_fusion.2
  431.4 8.5 multiply_reduce_fusion.12
  451.9 8.0 multiply_reduce_fusion.11
  460.1 9.2 subtract_reduce_fusion.2
  469.3 8.5 multiply_reduce_fusion.12
  489.8 8.0 multiply_reduce_fusion.11
  498.0 9.2 subtract_reduce_fusion.2
  507.2 8.5 multiply_reduce_fusion.12
  527.7 8.0 multiply_reduce_fusion.11
  535.9 9.2 subtract_reduce_fusion.2
  545.1 8.5 multiply_reduce_fusion.12
  565.6 8.0 multiply_reduce_fusion.11
  573.8 9.2 subtract_reduce_fusion.2
  583.0 8.5 multiply_reduce_fusion.12
  611.6 9.2 subtract_reduce_fusion.2
  620.8 8.5 multiply_reduce_fusion.12
  649.5 9.2 subtract_reduce_fusion.2
  658.7 8.5 multiply_reduce_fusion.12
  687.4 9.2 subtract_reduce_fusion.2
  696.6 8.5 multiply_reduce_fusion.12
  725.3 9.2 subtract_reduce_fusion.2
  734.5 8.5 multiply_reduce_fusion.12
  763.2 9.2 subtract_reduce_fusion.2
  772.4 8.5 multiply_reduce_fusion.12
  801.0 9.2 subtract_reduce_fusion.2
  810.2 8.5 multiply_reduce_fusion.12
  838.9 9.2 subtract_reduce_fusion.2
  848.1 8.5 multiply_reduce_fusion.12
  861.9 11.0 %collective-permute-done.1 = f32[192,512]{1,0:T(8,128)S(1)} collective-permute-done((f32[192,512]{1,0:T(8,128)S(1)}, f32[192,512]{1,0:T(8,128)S(1)}, u32[]{:S(2)}, u32[]{:S(2)}) %collective-permute-start.1) | collective-permute-done | bytes 393248 | tf_op jit(solution)/shard_map/ppermute | solution.py:15
  877.8 69.2 %while.27 = (s32[]{:T(128)}, f32[8,16,4,128]{3,2,1,0:T(4,128)S(1)}, f32[8,16,9,128]{3,1,0,2:T(8,128)}, s32[]{:T(128)}) while((s32[]{:T(128)}, f32[8,16,4,128]{3,2,1,0:T(4,128)S(1)}, f32[8,16,9,128]{3,1,0,2:T(8,128)}, s32[]{:T(128)}) %tuple.100), condition=%wide.region_14.15_spmd, body=%wide.region_9.14_spmd.sunk | while | flops 18925568 | bytes 11239485 | solution.py:148
  947.0 14.0 %reduce-scatter.2.cloned.1.call-done = f32[128,512]{1,0:T(8,128)} async-done(((f32[2048,512]{1,0:T(8,128)}), f32[128,512]{1,0:T(8,128)}) %reduce-scatter.2.cloned.1.call-update) | async-done | bytes 262160 | tf_op jit(solution)/shard_map/reduce_scatter | solution.py:137
  (661 shorter events, 355.7 us)
Async XLA Ops:
  16.7 196.1 %all-to-all-start = ((f32[16,128,9,128]{3,1,2,0:T(8,128)}), f32[16,128,9,128]{3,1,2,0:T(8,128)}, u32[]{:S(2)}, u32[]{:S(2)}) async-start(f32[16,128,9,128]{3,1,2,0:T(8,128)} %stack.2), calls=%async_computation | async-start | bytes 18874368 | tf_op jit(solution)/shard_map/all_to_all | solution.py:96
  25.0 936.1 %reduce-scatter.2.cloned.1.call-start = ((), (), s32[]{:S(2)}) async-start(), calls=%async_computation.2 | async-start | bytes 4456448 | tf_op jit(solution)/shard_map/reduce_scatter | solution.py:137
  239.7 9.2 copy-start.8
  247.4 3.5 collective-permute-start
  279.9 8.6 copy-start.5
  279.9 8.6 copy-start.7
  279.9 10.1 %copy-start = (f32[192,512]{1,0:T(8,128)S(1)}, f32[192,512]{1,0:T(8,128)}, u32[]{:S(2)}) copy-start(f32[192,512]{1,0:T(8,128)} %get-tuple-element.376) | copy-start | bytes 1179652 | tf_op jit(solution)/shard_map/while
  317.8 8.6 copy-start.5
  317.8 8.6 copy-start.7
  317.8 10.1 %copy-start = (f32[192,512]{1,0:T(8,128)S(1)}, f32[192,512]{1,0:T(8,128)}, u32[]{:S(2)}) copy-start(f32[192,512]{1,0:T(8,128)} %get-tuple-element.376) | copy-start | bytes 1179652 | tf_op jit(solution)/shard_map/while
  355.7 8.6 copy-start.5
  355.7 8.6 copy-start.7
  355.7 10.1 %copy-start = (f32[192,512]{1,0:T(8,128)S(1)}, f32[192,512]{1,0:T(8,128)}, u32[]{:S(2)}) copy-start(f32[192,512]{1,0:T(8,128)} %get-tuple-element.376) | copy-start | bytes 1179652 | tf_op jit(solution)/shard_map/while
  393.5 8.6 copy-start.5
  393.5 8.6 copy-start.7
  393.6 10.1 %copy-start = (f32[192,512]{1,0:T(8,128)S(1)}, f32[192,512]{1,0:T(8,128)}, u32[]{:S(2)}) copy-start(f32[192,512]{1,0:T(8,128)} %get-tuple-element.376) | copy-start | bytes 1179652 | tf_op jit(solution)/shard_map/while
  431.4 8.6 copy-start.5
  431.4 8.6 copy-start.7
  431.4 10.1 %copy-start = (f32[192,512]{1,0:T(8,128)S(1)}, f32[192,512]{1,0:T(8,128)}, u32[]{:S(2)}) copy-start(f32[192,512]{1,0:T(8,128)} %get-tuple-element.376) | copy-start | bytes 1179652 | tf_op jit(solution)/shard_map/while
  469.3 8.6 copy-start.5
  469.3 8.6 copy-start.7
  469.3 10.1 %copy-start = (f32[192,512]{1,0:T(8,128)S(1)}, f32[192,512]{1,0:T(8,128)}, u32[]{:S(2)}) copy-start(f32[192,512]{1,0:T(8,128)} %get-tuple-element.376) | copy-start | bytes 1179652 | tf_op jit(solution)/shard_map/while
  507.2 8.6 copy-start.5
  507.2 8.6 copy-start.7
  507.2 10.1 %copy-start = (f32[192,512]{1,0:T(8,128)S(1)}, f32[192,512]{1,0:T(8,128)}, u32[]{:S(2)}) copy-start(f32[192,512]{1,0:T(8,128)} %get-tuple-element.376) | copy-start | bytes 1179652 | tf_op jit(solution)/shard_map/while
  545.1 8.6 copy-start.5
  545.1 8.6 copy-start.7
  545.1 10.1 %copy-start = (f32[192,512]{1,0:T(8,128)S(1)}, f32[192,512]{1,0:T(8,128)}, u32[]{:S(2)}) copy-start(f32[192,512]{1,0:T(8,128)} %get-tuple-element.376) | copy-start | bytes 1179652 | tf_op jit(solution)/shard_map/while
  582.9 8.6 copy-start.5
  582.9 8.6 copy-start.7
  583.0 10.1 %copy-start = (f32[192,512]{1,0:T(8,128)S(1)}, f32[192,512]{1,0:T(8,128)}, u32[]{:S(2)}) copy-start(f32[192,512]{1,0:T(8,128)} %get-tuple-element.376) | copy-start | bytes 1179652 | tf_op jit(solution)/shard_map/while
  620.8 8.6 copy-start.5
  620.8 8.6 copy-start.7
  620.8 10.1 %copy-start = (f32[192,512]{1,0:T(8,128)S(1)}, f32[192,512]{1,0:T(8,128)}, u32[]{:S(2)}) copy-start(f32[192,512]{1,0:T(8,128)} %get-tuple-element.376) | copy-start | bytes 1179652 | tf_op jit(solution)/shard_map/while
  658.7 8.6 copy-start.5
  658.7 8.6 copy-start.7
  658.7 10.1 %copy-start = (f32[192,512]{1,0:T(8,128)S(1)}, f32[192,512]{1,0:T(8,128)}, u32[]{:S(2)}) copy-start(f32[192,512]{1,0:T(8,128)} %get-tuple-element.376) | copy-start | bytes 1179652 | tf_op jit(solution)/shard_map/while
  696.6 8.6 copy-start.5
  696.6 8.6 copy-start.7
  696.6 10.1 %copy-start = (f32[192,512]{1,0:T(8,128)S(1)}, f32[192,512]{1,0:T(8,128)}, u32[]{:S(2)}) copy-start(f32[192,512]{1,0:T(8,128)} %get-tuple-element.376) | copy-start | bytes 1179652 | tf_op jit(solution)/shard_map/while
  734.5 8.6 copy-start.5
  734.5 10.1 %copy-start = (f32[192,512]{1,0:T(8,128)S(1)}, f32[192,512]{1,0:T(8,128)}, u32[]{:S(2)}) copy-start(f32[192,512]{1,0:T(8,128)} %get-tuple-element.376) | copy-start | bytes 1179652 | tf_op jit(solution)/shard_map/while
  772.3 8.6 copy-start.5
  772.3 8.6 copy-start.7
  772.4 10.1 %copy-start = (f32[192,512]{1,0:T(8,128)S(1)}, f32[192,512]{1,0:T(8,128)}, u32[]{:S(2)}) copy-start(f32[192,512]{1,0:T(8,128)} %get-tuple-element.376) | copy-start | bytes 1179652 | tf_op jit(solution)/shard_map/while
  810.2 10.1 %copy-start = (f32[192,512]{1,0:T(8,128)S(1)}, f32[192,512]{1,0:T(8,128)}, u32[]{:S(2)}) copy-start(f32[192,512]{1,0:T(8,128)} %get-tuple-element.376) | copy-start | bytes 1179652 | tf_op jit(solution)/shard_map/while
  848.1 10.1 %copy-start = (f32[192,512]{1,0:T(8,128)S(1)}, f32[192,512]{1,0:T(8,128)}, u32[]{:S(2)}) copy-start(f32[192,512]{1,0:T(8,128)} %get-tuple-element.376) | copy-start | bytes 1179652 | tf_op jit(solution)/shard_map/while
  859.5 13.4 %collective-permute-start.1 = (f32[192,512]{1,0:T(8,128)S(1)}, f32[192,512]{1,0:T(8,128)S(1)}, u32[]{:S(2)}, u32[]{:S(2)}) collective-permute-start(f32[192,512]{1,0:T(8,128)S(1)} %slice.109), channel_id=1, source_target_pairs={{16,0},{32,16},{48,32},{64,48},{80,64},{96,80},{112,96},{17,1},{33... | collective-permute-start | bytes 1179656 | tf_op jit(solution)/shard_map/ppermute | solution.py:15
  (71 other events, 185.2 us)
Sparse Core Ops, SparseCore 0:
  877.9 83.1 reduce-scatter.1
